TPU v7x, 512 devices: a whole 4x4x16 slice. The times are simulated.
512 devices in a mesh: row: 32 (over z, y_hi), col: 16 (over x, y_lo, core).
Axes of the slice: x: 4, y: 4 (y_hi: 2, y_lo: 2; y = y_hi * 2 + y_lo), z: 16, core: 2. Of those that a mesh axis runs over, the one named last changes fastest.
Arguments:
- factor_band: float32 [4096, 131072], P('row', 'col'), may hold values from -0.015625 to 0.015625
- normals: float32 [131072, 384], P('col', 'row'), may hold values from -6 to 6
- site_mean: float32 [4096], P('row'), may hold values from 5 to 10
- site_spread: float32 [4096], P('row'), may hold values from 1 to 4
- site_capacity: float32 [4096], P('row'), may hold values from 0.1 to 1
- site_kind: int32 [4096], P('row'), may hold values 0 or 1
- site_plant: int32 [4096], P('row'), may hold values from 0 to 2047
Outputs:
- plant_output: float32 [384, 2048], P('col', 'row')
All inputs are finite; a program needn't handle non-finite values. No bound on the sum of `site_kind` on one device may be relied on, other than what follows from the above.
Results may differ from a plain program's by a relative error of at most 0.000096.
Values sent between devices are 32-bit elements; how exact they have to be, the bound alone decides.
A program may use at most 128 MiB of HBM per device.

v0:
```python
import jax
import jax.numpy as jnp
from jax import lax
from jax.sharding import PartitionSpec as P

PLANTS = 2048


def body(factor_band, normals, site_mean, site_spread, site_capacity, site_kind, site_plant):
    share = normals.shape[1] * lax.axis_size("row") // lax.axis_size("col")
    partial_rows = lax.dot_general(
        lax.all_gather(normals, "row", axis=1, tiled=True),
        factor_band,
        (((0,), (1,)), ((), ())),
        precision=lax.Precision.HIGHEST,
        preferred_element_type=jnp.float32,
    )
    total = lax.psum(partial_rows, "col")
    samples = lax.dynamic_slice_in_dim(total, lax.axis_index("col") * share, share, 0)
    speed = site_mean[None, :] + site_spread[None, :] * samples
    positive = jnp.maximum(speed, 0.0)
    wind = jnp.clip((positive * positive * positive - 27.0) / (1728.0 - 27.0), 0.0, 1.0)
    solar = jnp.clip(speed / 12.0, 0.0, 1.0)
    power = jnp.where(site_kind[None, :] == 1, solar, wind) * site_capacity[None, :]
    onehot = (site_plant[:, None] == jnp.arange(PLANTS, dtype=jnp.int32)[None, :]).astype(
        jnp.float32
    )
    terms = jnp.dot(
        power, onehot, precision=lax.Precision.HIGHEST, preferred_element_type=jnp.float32
    )
    return lax.psum_scatter(terms, "row", scatter_dimension=1, tiled=True)


def solution(mesh):
    in_specs = (P("row", "col"), P("col", "row"), P("row"), P("row"), P("row"), P("row"), P("row"))
    out_specs = P("col", "row")
    return jax.shard_map(body, mesh=mesh, in_specs=in_specs, out_specs=out_specs, check_vma=False)
```

profile of v0, /device:TPU:2, one launch (start us, length us, event | category | flops | bytes accessed | tf_op | source)
XLA Modules:
  0.0 1105.5 jit_solution(14875359424413770468)
XLA Ops:
  6.5 0.0 all-gather.3.cloned.1.call-start
  6.5 0.7 all-gather.3.cloned.1.call-update
  7.3 0.0 all-reduce.2.cloned.1.call-start
  7.3 275.4 %all-gather.3.cloned.1.call-done = f32[32,12,8192]{2,1,0:T(8,128)} async-done(((f32[1,12,8192]{2,1,0:T(8,128)}), f32[32,12,8192]{2,1,0:T(8,128)}) %all-gather.3.cloned.1.call-update) | async-done | bytes 12582928 | tf_op jit(solution)/shard_map/all_gather | solution.py:12
  282.7 12.5 %reshape.7 = f32[384,8192]{1,0:T(8,128)} reshape(f32[32,12,8192]{2,1,0:T(8,128)} %all-gather.3.cloned.1.call-done) | data formatting | bytes 25165824
  295.2 0.0 copy-start.4
  295.2 0.0 copy-start
  295.2 0.0 copy-start.1
  295.2 0.0 copy-start.2
  295.2 0.0 copy-start.3
  295.2 14.2 %fusion.28 = f32[384,128]{1,0:T(8,128)} fusion(f32[384,8192]{1,0:T(8,128)} %reshape.7, f32[128,8192]{1,0:T(8,128)} %param.7), kind=kOutput, calls=%fused_computation.31 | convolution fusion | flops 4831838208 | bytes 16973824 | tf_op jit(solution)/shard_map/dot_general | solution.py:11
  309.4 0.0 all-reduce.2.cloned.1.call-update
  309.5 0.0 reduce-scatter.4.cloned.1.call-start
  309.5 0.0 copy-done.4
  309.5 121.3 %all-reduce.2.cloned.1.call-done = f32[384,128]{1,0:T(8,128)} async-done(((f32[384,128]{1,0:T(8,128)}), f32[384,128]{1,0:T(8,128)}) %all-reduce.2.cloned.1.call-update) | async-done | bytes 196624 | tf_op jit(solution)/shard_map/psum | solution.py:18
  430.8 0.0 copy-done
  430.8 0.0 copy-done.1
  430.8 0.0 copy-done.2
  430.8 0.0 copy-done.3
  430.8 2.7 convolution_bitcast_fusion
  433.5 0.0 reduce-scatter.4.cloned.1.call-update
  433.6 663.9 %reduce-scatter.4.cloned.1.call-done = f32[64,24]{1,0:T(8,128)} async-done(((f32[2048,24]{1,0:T(8,128)}), f32[64,24]{1,0:T(8,128)}) %reduce-scatter.4.cloned.1.call-update) | async-done | bytes 6160
  1097.5 1.4 copy.9
  (1 shorter events, 0.0 us)
Async XLA Ops:
  6.5 276.2 %all-gather.3.cloned.1.call-start = ((), (), s32[]{:S(2)}) async-start(), calls=%async_computation.2 | async-start | bytes 17301504 | tf_op jit(solution)/shard_map/all_gather | solution.py:12
  7.3 423.5 %all-reduce.2.cloned.1.call-start = ((), (), s32[]{:S(2)}) async-start(), calls=%async_computation.1 | async-start | bytes 393216 | tf_op jit(solution)/shard_map/psum | solution.py:18
  295.2 14.3 %copy-start.4 = (s32[128]{0:T(128)S(1)}, s32[128]{0:T(128)}, u32[]{:S(2)}) copy-start(s32[128]{0:T(128)} %param.12) | copy-start | bytes 1540
  295.2 135.6 %copy-start = (s32[128]{0:T(128)S(1)}, s32[128]{0:T(128)}, u32[]{:S(2)}) copy-start(s32[128]{0:T(128)} %param.13) | copy-start | bytes 1540
  295.2 135.6 %copy-start.1 = (f32[128]{0:T(128)S(1)}, f32[128]{0:T(128)}, u32[]{:S(2)}) copy-start(f32[128]{0:T(128)} %param.11) | copy-start | bytes 1540
  295.2 135.6 %copy-start.2 = (f32[128]{0:T(128)S(1)}, f32[128]{0:T(128)}, u32[]{:S(2)}) copy-start(f32[128]{0:T(128)} %param.10) | copy-start | bytes 1540
  295.2 135.6 %copy-start.3 = (f32[128]{0:T(128)S(1)}, f32[128]{0:T(128)}, u32[]{:S(2)}) copy-start(f32[128]{0:T(128)} %param.9) | copy-start | bytes 1540
  309.5 788.1 %reduce-scatter.4.cloned.1.call-start = ((), (), s32[]{:S(2)}) async-start(), calls=%async_computation.3 | async-start | bytes 1081344
Sparse Core Ops, SparseCore 0:
  10.5 272.1 all-gather.2
  309.6 121.1 all-reduce.1
  435.8 661.6 reduce-scatter.3
where the time goes:
time: 1110 us
  waiting for transfers between devices  1060 us (95%)
  matrix products  17 us (2%)
  local copies, waits for them, and re-layouts  13.9 us (1%)
  between operations  13.1 us (1%)
    unnamed x4, waiting for transfers between devices  665 us
    all_gather x1, waiting for transfers between devices, body(): lax.all_gather(normals, 'row', axis=1, tiled=True)  275 us
    psum x1, waiting for transfers between devices, body(): total = lax.psum(partial_rows, 'col')  121 us
  transfers between devices with their start and end apart: 3, of which 3 were waited for; matrix products, arithmetic and copies ran while one was open for 0% of the time, Pallas kernels for 0%

commit v1 on v0

--- a/solution.py
+++ b/solution.py
@@ -15,7 +15,7 @@
         precision=lax.Precision.HIGHEST,
         preferred_element_type=jnp.float32,
     )
-    total = lax.psum(partial_rows, "col")
+    total = jnp.sum(lax.all_gather(partial_rows, "col"), axis=0)
     samples = lax.dynamic_slice_in_dim(total, lax.axis_index("col") * share, share, 0)
     speed = site_mean[None, :] + site_spread[None, :] * samples
     positive = jnp.maximum(speed, 0.0)

time: 1110 us -> 1020 us (0.919)
  the two profiles are of different devices: /device:TPU:2 before, /device:TPU:6 now
where the time goes in v1:
time: 1020 us
  waiting for transfers between devices  978 us (96%)
  matrix products  16.3 us (2%)
  local copies, waits for them, and re-layouts  13.9 us (1%)
  between operations  13.2 us (1%)
    unnamed x4, waiting for transfers between devices  664 us
    all_gather x1, waiting for transfers between devices, body(): lax.all_gather(normals, 'row', axis=1, tiled=True)  275 us
    all_gather x1, waiting for transfers between devices, body(): total = jnp.sum(lax.all_gather(partial_rows, 'col'), axis=0)  38.8 us
  transfers between devices with their start and end apart: 3, of which 3 were waited for; matrix products, arithmetic and copies ran while one was open for 0% of the time, Pallas kernels for 0%

profile of v1, /device:TPU:6, one launch (start us, length us, event | category | flops | bytes accessed | tf_op | source)
XLA Modules:
  0.0 1023.2 jit_solution(15574426450317042538)
XLA Ops:
  6.5 0.0 all-gather.7.cloned.1.call-start
  6.5 0.7 all-gather.7.cloned.1.call-update
  7.3 0.0 all-gather.5.cloned.1.call-start
  7.3 275.4 %all-gather.7.cloned.1.call-done = f32[32,12,8192]{2,1,0:T(8,128)} async-done(((f32[1,12,8192]{2,1,0:T(8,128)}), f32[32,12,8192]{2,1,0:T(8,128)}) %all-gather.7.cloned.1.call-update) | async-done | bytes 12582928 | tf_op jit(solution)/shard_map/all_gather | solution.py:12
  282.7 12.5 %reshape.8 = f32[384,8192]{1,0:T(8,128)} reshape(f32[32,12,8192]{2,1,0:T(8,128)} %all-gather.7.cloned.1.call-done) | data formatting | bytes 25165824
  295.1 0.0 copy-start.4
  295.1 0.0 copy-start
  295.2 0.0 copy-start.1
  295.2 0.0 copy-start.2
  295.2 0.0 copy-start.3
  295.2 14.2 %fusion.28 = f32[384,128]{1,0:T(8,128)} fusion(f32[384,8192]{1,0:T(8,128)} %reshape.8, f32[128,8192]{1,0:T(8,128)} %param.7), kind=kOutput, calls=%fused_computation.31 | convolution fusion | flops 4831838208 | bytes 16973824 | tf_op jit(solution)/shard_map/dot_general | solution.py:11
  309.4 0.0 all-gather.5.cloned.1.call-update
  309.4 0.0 reduce-scatter.4.cloned.1.call-start
  309.5 0.0 copy-done.4
  309.5 38.8 %all-gather.5.cloned.1.call-done = f32[6144,128]{1,0:T(8,128)} async-done(((f32[384,128]{1,0:T(8,128)}), f32[6144,128]{1,0:T(8,128)}) %all-gather.5.cloned.1.call-update) | async-done | bytes 3145744 | tf_op jit(solution)/shard_map/all_gather | solution.py:18
  348.3 2.1 reduce_sum.9
  350.3 0.0 copy-done
  350.3 0.0 copy-done.1
  350.3 0.0 copy-done.2
  350.3 0.0 copy-done.3
  350.3 2.0 convolution_bitcast_fusion
  352.4 0.0 reduce-scatter.4.cloned.1.call-update
  352.4 662.8 %reduce-scatter.4.cloned.1.call-done = f32[64,24]{1,0:T(8,128)} async-done(((f32[2048,24]{1,0:T(8,128)}), f32[64,24]{1,0:T(8,128)}) %reduce-scatter.4.cloned.1.call-update) | async-done | bytes 6160
  1015.3 1.4 copy.9
  (1 shorter events, 0.0 us)
Async XLA Ops:
  6.5 276.1 %all-gather.7.cloned.1.call-start = ((), (), s32[]{:S(2)}) async-start(), calls=%async_computation.2 | async-start | bytes 17301504 | tf_op jit(solution)/shard_map/all_gather | solution.py:12
  7.3 341.0 %all-gather.5.cloned.1.call-start = ((), (), s32[]{:S(2)}) async-start(), calls=%async_computation.1 | async-start | bytes 3342336 | tf_op jit(solution)/shard_map/all_gather | solution.py:18
  295.1 14.3 %copy-start.4 = (s32[128]{0:T(128)S(1)}, s32[128]{0:T(128)}, u32[]{:S(2)}) copy-start(s32[128]{0:T(128)} %param.12) | copy-start | bytes 1540
  295.1 55.2 %copy-start = (s32[128]{0:T(128)S(1)}, s32[128]{0:T(128)}, u32[]{:S(2)}) copy-start(s32[128]{0:T(128)} %param.13) | copy-start | bytes 1540
  295.2 55.2 %copy-start.1 = (f32[128]{0:T(128)S(1)}, f32[128]{0:T(128)}, u32[]{:S(2)}) copy-start(f32[128]{0:T(128)} %param.11) | copy-start | bytes 1540
  295.2 55.2 %copy-start.2 = (f32[128]{0:T(128)S(1)}, f32[128]{0:T(128)}, u32[]{:S(2)}) copy-start(f32[128]{0:T(128)} %param.10) | copy-start | bytes 1540
  295.2 55.2 %copy-start.3 = (f32[128]{0:T(128)S(1)}, f32[128]{0:T(128)}, u32[]{:S(2)}) copy-start(f32[128]{0:T(128)} %param.9) | copy-start | bytes 1540
  309.4 705.8 %reduce-scatter.4.cloned.1.call-start = ((), (), s32[]{:S(2)}) async-start(), calls=%async_computation.3 | async-start | bytes 1081344
Sparse Core Ops, SparseCore 0:
  10.5 272.1 all-gather.6
  309.5 38.6 all-gather.4
  352.6 662.5 reduce-scatter.3
